TPU v7x, 32 devices: a whole 2x2x4 slice. The times are simulated.
32 devices in a mesh: dp: 4 (over x, core), expert: 8 (over z, y).
Axes of the slice: x: 2, y: 2, z: 4, core: 2. Of those that a mesh axis runs over, the one named last changes fastest.
Arguments:
- tokens: bfloat16 [32768, 768], P(('dp', 'expert')), may hold values from -6 to 6
- segments: int32 [32, 1024], P(('dp', 'expert')), may hold values from 0 to 7, never falling along the last dimension, each value on 1 to 512 neighbouring positions
- routes: int32 [32768, 1], P(('dp', 'expert')), may hold values from 0 to 7
- cotangent: bfloat16 [32768, 768], P(('dp', 'expert')), may hold values from -6 to 6
- attn_gain: float32 [768], replicated, may hold values from 0.5 to 1.5
- ffn_gain: float32 [768], replicated, may hold values from 0.5 to 1.5
- query_weight: bfloat16 [768, 768], replicated, may hold values from -0.21875 to 0.21875
- key_weight: bfloat16 [768, 768], replicated, may hold values from -0.21875 to 0.21875
- value_weight: bfloat16 [768, 768], replicated, may hold values from -0.21875 to 0.21875
- output_weight: bfloat16 [768, 768], replicated, may hold values from -0.875 to 0.875
- position_bias_grid: float32 [32, 12], replicated, may hold values from -6 to 6
- router_weight: float32 [768, 8], replicated, may hold values from -0.15625 to 0.15625
- expert_in: bfloat16 [8, 768, 3072], P('expert'), may hold values from -0.21875 to 0.21875
- expert_out: bfloat16 [8, 3072, 768], P('expert'), may hold values from -0.875 to 0.875
Outputs:
- mixed: bfloat16 [32768, 768], P(('dp', 'expert'))
- grad_tokens: bfloat16 [32768, 768], P(('dp', 'expert'))
- grad_attn_gain: float32 [768], replicated
- grad_ffn_gain: float32 [768], replicated
- grad_query: float32 [768, 768], replicated
- grad_key: float32 [768, 768], replicated
- grad_value: float32 [768, 768], replicated
- grad_output: float32 [768, 768], replicated
- grad_bias: float32 [32, 12], replicated
- grad_router: float32 [768, 8], replicated
- grad_expert_in: float32 [8, 768, 3072], P('expert', None, 'dp')
- grad_expert_out: float32 [8, 3072, 768], P('expert', 'dp')
All inputs are finite; a program needn't handle non-finite values.
Results may differ from a plain program's by a relative error of at most 0.017.
Values may be sent and summed in bfloat16 or wider, within the bound.
A program may use at most 320 MiB of HBM per device.

v0:
```python
import functools

import jax
import jax.numpy as jnp
from jax import lax
from jax.experimental import pallas as pl
from jax.experimental.pallas import tpu as pltpu
from jax.sharding import PartitionSpec as P

epsilon = 1e-06
precise_setting = lax.Precision.HIGHEST
def matmul(left, right):
    return jnp.dot(left, right, preferred_element_type=jnp.float32)


def matmul_tn(left, right):
    return lax.dot_general(left, right, (((0,), (0,)), ((), ())), preferred_element_type=jnp.float32)


def matmul_nt(left, right):
    return lax.dot_general(left, right, (((1,), (1,)), ((), ())), preferred_element_type=jnp.float32)


bucket_bounds = (12, 16, 23, 32, 46, 64, 91)
masked_score = -1e30
LANES = 128
BLOCK = 128
NEAR = 5
UF = 6
UB = 6


def bucket_of(relative):
    distance = jnp.abs(relative)
    beyond = jnp.zeros_like(distance)
    for threshold in bucket_bounds:
        beyond = beyond + (distance >= threshold).astype(jnp.int32)
    inside = jnp.where(distance < 8, distance, 8 + beyond)
    return inside + 16 * (relative > 0).astype(jnp.int32)


def dot_nt(a, b):
    return lax.dot_general(a, b, (((1,), (1,)), ((), ())), preferred_element_type=jnp.float32)


def dot_nn(a, b):
    return lax.dot_general(a, b, (((1,), (0,)), ((), ())), preferred_element_type=jnp.float32)


def split3(x):
    a = x.astype(jnp.bfloat16)
    r = x - a.astype(jnp.float32)
    b = r.astype(jnp.bfloat16)
    c = (r - b.astype(jnp.float32)).astype(jnp.bfloat16)
    return a, b, c


def fill_bias(diag_ref, bias, pairs):
    for p in range(pairs):
        for d in range(NEAR):
            tiles = []
            for h in (2 * p, 2 * p + 1):
                row = diag_ref[h : h + 1, :]
                if d in (0, NEAR - 1):
                    col = row[:, 511:512] if d == 0 else row[:, 0:1]
                    tiles.append(jnp.broadcast_to(col, (BLOCK, BLOCK)))
                else:
                    base = (3 - d) * BLOCK
                    wide = jnp.broadcast_to(row[:, base : base + 2 * BLOCK], (BLOCK, 2 * BLOCK))
                    tiles.append(pltpu.roll(wide, BLOCK, 1, stride=1, stride_axis=0)[:, :BLOCK])
            bias[p, d] = jnp.concatenate(tiles, 1)


def heads_apart(block, low, extra=None):
    zero = jnp.zeros_like(block)
    first, second = jnp.where(low, block, zero), jnp.where(low, zero, block)
    if extra is not None:
        first, second = jnp.concatenate([first, extra], 1), jnp.concatenate([second, extra], 1)
    return jnp.concatenate([first, second], 0)


def by_count(lo, hi, most, body):
    for n in range(1, most + 1):
        pl.when(hi - lo == n)(functools.partial(body, n))


def own_heads(wide):
    return jnp.concatenate([wide[:64, :LANES], wide[64:128, LANES:]], 0)


def attend(lo_ref, hi_ref, q_ref, k_ref, vt_ref, qm_ref, km_ref, bias, o_ref, lse_ref):
    pairs = q_ref.shape[1] // LANES
    length = q_ref.shape[0]
    nblk = length // BLOCK
    f32, bf16 = jnp.float32, jnp.bfloat16
    low = lax.broadcasted_iota(jnp.int32, (1, LANES), 1) < 64

    def q_block(i, _):
        lo, hi = lo_ref[i], hi_ref[i]
        rows = pl.ds(pl.multiple_of(i * BLOCK, BLOCK), BLOCK)
        start = pl.multiple_of(lo * BLOCK, BLOCK)
        qm = qm_ref[rows, :]

        def body(n):
            span = pl.ds(start, n * BLOCK)
            km = km_ref[span, :]

            def lanes_of(p):
                return pl.ds(pl.multiple_of(p * LANES, LANES), LANES)

            def scores(p):
                qs = heads_apart(q_ref[rows, lanes_of(p)], low, qm)
                return dot_nt(jnp.concatenate([k_ref[span, lanes_of(p)], km], 1), qs)

            def soften(p, st):
                parts = []
                top = None
                for b in range(n):
                    d = jnp.clip(lo + b - i, -2, 2) + 2
                    s = st[b * BLOCK : (b + 1) * BLOCK] + bias[p, d]
                    parts.append(s)
                    top = s if top is None else jnp.maximum(top, s)
                top = jnp.max(top, 0, keepdims=True)
                return jnp.concatenate([jnp.exp(s - top).astype(bf16) for s in parts], 0), top

            def mix(p, probs):
                values = jnp.concatenate([vt_ref[lanes_of(p), span], jnp.ones((16, n * BLOCK), bf16)], 0)
                return dot_nn(values, probs)

            def finish(p, acc, top):
                total = acc[LANES : LANES + 1]
                inv = 1.0 / total
                ot = own_heads(acc)
                ot = jnp.concatenate([ot[:64] * inv[:, :LANES], ot[64:] * inv[:, LANES:]], 0)
                o_ref[rows, lanes_of(p)] = ot.T.astype(bf16)
                lse_ref[i, pl.ds(p, 1), :] = top + jnp.log(total)

            def some(g, _):
                ps = [g * UF + u for u in range(UF)]
                sts = [scores(p) for p in ps]
                soft = [soften(p, st) for p, st in zip(ps, sts)]
                accs = [mix(p, x[0]) for p, x in zip(ps, soft)]
                for p, acc, x in zip(ps, accs, soft):
                    finish(p, acc, x[1])
                return 0
            lax.fori_loop(0, pairs // UF, some, 0)

        by_count(lo, hi, nblk, body)
        return 0
    lax.fori_loop(0, nblk, q_block, 0)


def attend_back(
    lo_ref, hi_ref, q_ref, k_ref, kt_ref, v_ref, lse_ref, do_ref, o_ref, qm_ref, km_ref, bias,
    dq_ref, dk_ref, dv_ref, gsum_ref, gacc, dkacc, dvacc, scale,
):
    length, width = q_ref.shape
    pairs = width // LANES
    nblk = length // BLOCK
    f32, bf16 = jnp.float32, jnp.bfloat16
    low = lax.broadcasted_iota(jnp.int32, (1, LANES), 1) < 64
    pick = (
        lax.broadcasted_iota(jnp.int32, (16, LANES), 0) == lax.broadcasted_iota(jnp.int32, (16, LANES), 1) // 64
    ).astype(f32).astype(bf16)
    gacc[...] = jnp.zeros_like(gacc)
    gsum_ref[...] = jnp.zeros_like(gsum_ref)
    dkacc[...] = jnp.zeros_like(dkacc)
    dvacc[...] = jnp.zeros_like(dvacc)

    def q_block(i, _):
        lo, hi = lo_ref[i], hi_ref[i]
        rows = pl.ds(pl.multiple_of(i * BLOCK, BLOCK), BLOCK)
        start = pl.multiple_of(lo * BLOCK, BLOCK)
        qm = qm_ref[rows, :]

        def body(n):
            span = pl.ds(start, n * BLOCK)
            km = km_ref[span, :]

            def lanes_of(p):
                return pl.ds(pl.multiple_of(p * LANES, LANES), LANES)

            def products(p):
                cols = lanes_of(p)
                qs = heads_apart(q_ref[rows, cols], low, qm)
                dd = do_ref[rows, cols]
                dos = heads_apart(dd, low)
                prod = dd.astype(f32) * o_ref[rows, cols].astype(f32)
                prod_hi = prod.astype(bf16)
                prod_lo = (prod - prod_hi.astype(f32)).astype(bf16)
                inner = dot_nt(pick, prod_hi) + dot_nt(pick, prod_lo)
                inner = jnp.concatenate([inner[0:1], inner[1:2]], 1)
                st = dot_nt(jnp.concatenate([k_ref[span, cols], km], 1), qs)
                dpt = dot_nt(v_ref[span, cols], dos)
                return qs, dos, inner, st, dpt

            def pointwise(p, inner, st, dpt):
                lse = lse_ref[i, pl.ds(p, 1), :]
                probs, grads = [], []
                for b in range(n):
                    d = jnp.clip(lo + b - i, -2, 2) + 2
                    part = slice(b * BLOCK, (b + 1) * BLOCK)
                    prob = jnp.exp(st[part] + bias[p, d] - lse)
                    grad = prob * (dpt[part] - inner)
                    gacc[p, d] += grad
                    probs.append(prob.astype(bf16))
                    grads.append(grad.astype(bf16))
                return jnp.concatenate(probs, 0), jnp.concatenate(grads, 0)

            def back(p, qs, dos, probs, grads):
                cols = lanes_of(p)
                return (
                    dot_nn(probs, dos), dot_nn(grads, qs[:, :LANES]), dot_nn(kt_ref[cols, span], grads)
                )

            def finish(p, dv, dk, dqt):
                cols = lanes_of(p)
                dvacc[span, cols] += dv
                dkacc[span, cols] += dk
                dq_ref[rows, cols] = (own_heads(dqt).T * scale).astype(bf16)

            def some(g, _):
                ps = [g * UB + u for u in range(UB)]
                first = [products(p) for p in ps]
                points = [pointwise(p, *x[2:]) for p, x in zip(ps, first)]
                last = [back(p, *x[:2], *y) for p, x, y in zip(ps, first, points)]
                for p, x in zip(ps, last):
                    finish(p, *x)
                return 0
            lax.fori_loop(0, pairs // UB, some, 0)

        by_count(lo, hi, nblk, body)
        return 0
    lax.fori_loop(0, nblk, q_block, 0)
    dk_ref[...] = dkacc[...].astype(bf16)
    dv_ref[...] = dvacc[...].astype(bf16)
    turn = (
        lax.broadcasted_iota(jnp.int32, (BLOCK, BLOCK), 0) + lax.broadcasted_iota(jnp.int32, (BLOCK, BLOCK), 1)
        == BLOCK - 1
    ).astype(f32).astype(bf16)
    for p in range(pairs):
        for d in range(NEAR):
            t = gacc[p, d]
            if 0 < d < NEAR - 1:
                hi = t.astype(bf16)
                t = dot_nn(turn, hi) + dot_nn(turn, (t - hi.astype(f32)).astype(bf16))
            for u in range(2):
                s = jnp.concatenate([t[:, u * LANES : (u + 1) * LANES], jnp.zeros((BLOCK, LANES), f32)], 1)
                if 0 < d < NEAR - 1:
                    s = pltpu.roll(s, 0, 1, stride=1, stride_axis=0)
                at = d * 16 + 2 * p + u
                gsum_ref[at : at + 1, :] = jnp.sum(s, 0, keepdims=True)


def two(x):
    a = x.astype(jnp.bfloat16)
    return a, (x - a.astype(jnp.float32)).astype(jnp.bfloat16)


def row_pieces(row):
    place = lax.broadcasted_iota(jnp.int32, (16, row.shape[1]), 0)
    a, b, c = [x.astype(jnp.float32) for x in split3(row)]
    return jnp.where(place == 0, a, jnp.where(place == 1, b, jnp.where(place == 2, c, 0.0))).astype(jnp.bfloat16)


def each(count, body):
    if count <= 8:
        for e in range(count):
            body(e)
    else:
        def step(e, _):
            body(e)
            return 0
        lax.fori_loop(0, count, step, 0)


def slot_hot(slot_row, e, slot_rows):
    place = lax.broadcasted_iota(jnp.int32, (slot_rows, slot_row.shape[1]), 0) + e * slot_rows
    return (place == slot_row).astype(jnp.float32).astype(jnp.bfloat16)


def slots_kernel(routes_ref, rows_ref, slot_ref, out_ref, *, experts, capacity, slot_rows):
    f32, bf16 = jnp.float32, jnp.bfloat16
    tokens = routes_ref.shape[1]
    routes = routes_ref[...]
    pad = max(experts, 16)
    hot = (lax.broadcasted_iota(jnp.int32, (pad, tokens), 0) == routes).astype(f32)
    earlier = (
        lax.broadcasted_iota(jnp.int32, (BLOCK, BLOCK), 0) < lax.broadcasted_iota(jnp.int32, (BLOCK, BLOCK), 1)
    ).astype(f32).astype(bf16)
    seen = jnp.zeros((pad, 1), f32)
    ranks = []
    for c in range(0, tokens, BLOCK):
        part = hot[:, c : c + BLOCK]
        ranks.append(jnp.sum((dot_nn(part.astype(bf16), earlier) + seen) * part, 0, keepdims=True))
        seen = seen + jnp.sum(part, 1, keepdims=True)
    rank = jnp.concatenate(ranks, 1).astype(jnp.int32)
    slot = jnp.where(rank < capacity, routes * slot_rows + rank, -1)
    slot_ref[...] = jnp.broadcast_to(slot, slot_ref.shape)

    def pair(e):
        rows = dot_nn(slot_hot(slot, e, 2 * slot_rows), rows_ref[...]).astype(bf16)
        out_ref[pl.ds(2 * e, 2)] = rows.reshape(2, slot_rows, rows.shape[1])
    each(experts // 2, pair)


def first_slots(routes_row, rows, experts, capacity, slot_rows):
    tokens, width = rows.shape
    vmem = pl.BlockSpec(memory_space=pltpu.VMEM)
    return pl.pallas_call(
        functools.partial(slots_kernel, experts=experts, capacity=capacity, slot_rows=slot_rows),
        out_shape=(
            jax.ShapeDtypeStruct((8, tokens), jnp.int32),
            jax.ShapeDtypeStruct((experts, slot_rows, width), jnp.bfloat16),
        ),
        in_specs=[vmem] * 2,
        out_specs=(vmem,) * 2,
        compiler_params=pltpu.CompilerParams(vmem_limit_bytes=63 << 20),
        cost_estimate=pl.CostEstimate(
            flops=2 * experts * slot_rows * tokens * width, bytes_accessed=4 << 20, transcendentals=0
        ),
    )(routes_row, rows)


def fill_masks(segment_row, qm, km):
    f32, bf16 = jnp.float32, jnp.bfloat16
    lane = lax.broadcasted_iota(jnp.int32, (1, LANES), 1)
    for b in range(qm.shape[0] // BLOCK):
        span = slice(b * BLOCK, (b + 1) * BLOCK)
        hot = (lax.broadcasted_iota(jnp.int32, (LANES, BLOCK), 0) == segment_row[:, span]).astype(f32).T
        qm[span, :] = (hot * masked_score).astype(bf16)
        km[span, :] = jnp.where(lane < 8, 1.0 - hot, 0.0).astype(bf16)


def fill_diag(grid_ref, diag, heads):
    bf16 = jnp.bfloat16
    buckets = grid_ref.shape[0]
    relative = 256 - lax.broadcasted_iota(jnp.int32, (buckets, 4 * LANES), 1)
    hot = (lax.broadcasted_iota(jnp.int32, (buckets, 4 * LANES), 0) == bucket_of(relative))
    hot = hot.astype(jnp.float32).astype(bf16)
    grid = jnp.concatenate(
        [grid_ref[...], jnp.zeros((buckets, LANES - heads), jnp.float32)], 1
    ).T[:16]
    total = None
    for piece in split3(grid):
        term = dot_nn(piece, hot)
        total = term if total is None else total + term
    diag[...] = total


def front_kernel(
    lo_ref, hi_ref, tokens, segment_row, slot_ref, routes_ref, gain_one, gain_two, wq, wk, wv, wo, grid_ref, router_t,
    q_ref, k_ref, kt_ref, v_ref, o_ref, lse_ref, middle_ref, probs_ref, xs_ref, gs_ref,
    vt_ref, qm_ref, km_ref, diag, bias, hidden, *, experts, slot_rows, scale,
):
    f32, bf16 = jnp.float32, jnp.bfloat16
    length, width = tokens.shape
    pairs = width // LANES
    nblk = length // BLOCK
    heads = grid_ref.shape[1]
    low = lax.broadcasted_iota(jnp.int32, (1, LANES), 1) < 64
    step = 256

    for b in range(length // step):
        span = slice(b * step, (b + 1) * step)
        x = tokens[span, :].astype(f32)
        inverse = lax.rsqrt(jnp.mean(x * x, 1, keepdims=True) + epsilon)
        normed = (x * inverse * gain_one[...]).astype(bf16)
        q_ref[span, :] = (dot_nn(normed, wq[...]).astype(bf16).astype(f32) * scale).astype(bf16)
        k = dot_nn(normed, wk[...]).astype(bf16)
        k_ref[span, :] = k
        kt_ref[:, span] = k.T
        v = dot_nn(normed, wv[...]).astype(bf16)
        v_ref[span, :] = v
        vt_ref[:, span] = v.T
    fill_masks(segment_row[...], qm_ref, km_ref)
    fill_diag(grid_ref, diag, heads)
    fill_bias(diag, bias, pairs)
    attend(lo_ref, hi_ref, q_ref, k_ref, vt_ref, qm_ref, km_ref, bias, o_ref, lse_ref)

    rw = two(router_t[...])
    routes = routes_ref[...]
    pad = router_t.shape[0]
    place = lax.broadcasted_iota(jnp.int32, (pad, step), 0)
    gates = []
    for b in range(length // step):
        span = slice(b * step, (b + 1) * step)
        middle = tokens[span, :].astype(f32) + dot_nn(o_ref[span, :], wo[...])
        middle_ref[span, :] = middle
        inverse = lax.rsqrt(jnp.mean(middle * middle, 1, keepdims=True) + epsilon)
        parts = two(middle * inverse * gain_two[...])
        hidden[span, :] = parts[0]
        logits = dot_nt(rw[0], parts[0]) + dot_nt(rw[0], parts[1]) + dot_nt(rw[1], parts[0])
        logits = jnp.where(place < experts, logits, -1e30)
        powers = jnp.exp(logits - jnp.max(logits, 0, keepdims=True))
        probs = powers / jnp.sum(powers, 0, keepdims=True)
        probs_ref[:, span] = probs
        gates.append(jnp.sum(jnp.where(place == routes[:, span], probs, 0.0), 0, keepdims=True))
    gates = row_pieces(jnp.concatenate(gates, 1))
    slot = slot_ref[0:1, :]
    lanes = gs_ref.shape[2]

    def one(e):
        hot = slot_hot(slot, e, slot_rows)
        xs_ref[e] = dot_nn(hot, hidden[...]).astype(bf16)
        if lanes > slot_rows:
            hot = jnp.concatenate([hot, jnp.zeros((lanes - slot_rows, length), bf16)], 0)
        row = jnp.sum(dot_nt(gates, hot), 0, keepdims=True)
        gs_ref[e] = jnp.broadcast_to(row, gs_ref.shape[1:])
    each(experts, one)


def front(lo, hi, tokens, segments, slot, routes_row, gain_one, gain_two, wq, wk, wv, wo, grid, router_t, experts, slot_rows, scale):
    length, width = tokens.shape
    heads = grid.shape[1]
    pairs = width // LANES
    nblk = length // BLOCK
    lanes = (slot_rows + LANES - 1) // LANES * LANES
    smem = pl.BlockSpec(memory_space=pltpu.SMEM)
    vmem = pl.BlockSpec(memory_space=pltpu.VMEM)
    f32, bf16 = jnp.float32, jnp.bfloat16
    shape = jax.ShapeDtypeStruct
    act = shape((length, width), bf16)
    return pl.pallas_call(
        functools.partial(front_kernel, experts=experts, slot_rows=slot_rows, scale=scale),
        out_shape=(
            act, act, shape((width, length), bf16), act, act,
            shape((nblk, 8, 2 * LANES), f32), shape((length, width), f32),
            shape((router_t.shape[0], length), f32),
            shape((experts, slot_rows, width), bf16), shape((experts, 8, lanes), f32),
        ),
        in_specs=[smem] * 2 + [vmem] * 12,
        out_specs=(vmem,) * 10,
        scratch_shapes=[
            pltpu.VMEM((width, length), bf16),
            pltpu.VMEM((length, LANES), bf16),
            pltpu.VMEM((length, LANES), bf16),
            pltpu.VMEM((16, 4 * LANES), f32),
            pltpu.VMEM((pairs, NEAR, BLOCK, 2 * LANES), f32),
            pltpu.VMEM((length, width), bf16),
        ],
        compiler_params=pltpu.CompilerParams(vmem_limit_bytes=63 << 20),
        cost_estimate=pl.CostEstimate(
            flops=4 * length * length * width + 12 * length * width * width, bytes_accessed=20 << 20,
            transcendentals=length * length * heads,
        ),
    )(lo, hi, tokens, segments, slot, routes_row, gain_one, gain_two, wq, wk, wv, wo, grid, router_t)


def bucket_sums(gsum_ref):
    bf16 = jnp.bfloat16
    total = jnp.zeros((16, LANES), jnp.float32)
    lane = lax.broadcasted_iota(jnp.int32, (2 * LANES, LANES), 1)
    for d in range(NEAR):
        relative = (d - 2) * BLOCK + BLOCK - 1 - lax.broadcasted_iota(jnp.int32, (2 * LANES, LANES), 0)
        bucket = 15 if d == 0 else 31 if d == NEAR - 1 else bucket_of(relative)
        hot = (lane == bucket).astype(jnp.float32).astype(bf16)
        for piece in split3(gsum_ref[d * 16 : (d + 1) * 16, :]):
            total = total + dot_nn(piece, hot)
    return total


def small_shape(width, experts):
    return (16 + width // LANES * experts + 16, LANES)


def back_kernel(
    lo_ref, hi_ref, home, home_gate, slot_ref, routes_ref, probs_ref, middle_ref, cotangent, segment_row, gain_two,
    wo, router_t, grid_ref, lse_ref, q_hbm, k_hbm, kt_hbm, v_hbm, o_hbm,
    dq_ref, dk_ref, dv_ref, middle_grad_hbm, small,
    q_ref, k_ref, kt_ref, v_ref, o_ref, middle_grad,
    do_ref, qm_ref, km_ref, diag, bias, gacc, dkacc, dvacc, logit, gsum_ref, sems,
    *, experts, slot_rows, scale,
):
    f32, bf16 = jnp.float32, jnp.bfloat16
    length, width = middle_ref.shape
    pairs = width // LANES
    pad = router_t.shape[0]
    heads = grid_ref.shape[1]
    slot = slot_ref[0:1, :]
    loads = [
        pltpu.make_async_copy(there, here, sems.at[i])
        for i, (there, here) in enumerate(zip(
            (q_hbm, k_hbm, kt_hbm, v_hbm, o_hbm), (q_ref, k_ref, kt_ref, v_ref, o_ref)))
    ]
    for load in loads:
        load.start()

    if experts <= 8:
        total = jnp.zeros((16, length), f32)
        for e in range(experts):
            total = total + dot_nn(row_pieces(home_gate[e, 0:1, :])[:, :slot_rows], slot_hot(slot, e, slot_rows))
    else:
        def add(e, total):
            return total + dot_nn(row_pieces(home_gate[e, 0:1, :])[:, :slot_rows], slot_hot(slot, e, slot_rows))
        total = lax.fori_loop(0, experts, add, jnp.zeros((16, length), f32))
    gate_grad = jnp.sum(total, 0, keepdims=True)
    place = lax.broadcasted_iota(jnp.int32, (pad, length), 0)
    hot = place == routes_ref[...]
    probs = probs_ref[...]
    gate = jnp.sum(jnp.where(hot, probs, 0.0), 0, keepdims=True)
    logit[...] = probs * (jnp.where(hot, gate_grad, 0.0) - gate * gate_grad)
    rw = two(router_t[...])
    slots = experts * slot_rows
    router_sum = jnp.zeros((pad, width), f32)
    gain_sum = jnp.zeros((1, width), f32)
    step = 256
    for b in range(length // step):
        span = slice(b * step, (b + 1) * step)
        hots = []
        for c in range(b * step, (b + 1) * step, BLOCK):
            column = jnp.broadcast_to(slot[:, c : c + BLOCK].astype(f32), (BLOCK, BLOCK)).T
            first = lax.broadcasted_iota(jnp.int32, (BLOCK, LANES), 1).astype(f32)
            hots.append(jnp.concatenate(
                [(column == first + float(s)).astype(f32).astype(bf16) for s in range(0, slots, LANES)], 1))
        spread = jnp.concatenate(hots, 0)
        hidden_grad = dot_nn(spread, home[...].reshape(slots, width))
        lg = two(logit[:, span])
        hidden_grad = hidden_grad + (
            matmul_tn(lg[0], rw[0]) + matmul_tn(lg[0], rw[1]) + matmul_tn(lg[1], rw[0])
        )
        middle = middle_ref[span, :]
        inverse = lax.rsqrt(jnp.mean(middle * middle, 1, keepdims=True) + epsilon)
        unit = middle * inverse
        hidden = two(unit * gain_two[...])
        router_sum = router_sum + (dot_nn(lg[0], hidden[0]) + dot_nn(lg[0], hidden[1]) + dot_nn(lg[1], hidden[0]))
        gain_sum = gain_sum + jnp.sum(hidden_grad * unit, 0, keepdims=True)
        scaled = hidden_grad * gain_two[...]
        mean = jnp.mean(scaled * middle, 1, keepdims=True)
        grad = cotangent[span, :].astype(f32) + inverse * (scaled - unit * (inverse * mean))
        middle_grad[span, :] = grad
        do_ref[span, :] = matmul_nt(grad.astype(bf16), wo[...]).astype(bf16)
    store = pltpu.make_async_copy(middle_grad, middle_grad_hbm, sems.at[5])
    store.start()
    small[...] = jnp.zeros_like(small)
    chunks = width // LANES
    for c in range(chunks):
        cols = slice(c * LANES, (c + 1) * LANES)
        small[8 + c : 9 + c, :] = gain_sum[:, cols]
        small[16 + c * experts : 16 + (c + 1) * experts, :] = router_sum[:experts, cols]

    fill_masks(segment_row[...], qm_ref, km_ref)
    fill_diag(grid_ref, diag, heads)
    fill_bias(diag, bias, pairs)
    for load in loads:
        load.wait()
    attend_back(
        lo_ref, hi_ref, q_ref, k_ref, kt_ref, v_ref, lse_ref, do_ref, o_ref, qm_ref, km_ref, bias,
        dq_ref, dk_ref, dv_ref, gsum_ref, gacc, dkacc, dvacc, scale,
    )
    at = 16 + chunks * experts
    small[at : at + 16, :] = bucket_sums(gsum_ref)
    store.wait()


def back(lo, hi, home, home_gate, slot, routes_row, probs, middle, cotangent, segments, gain_two, wo, router_t, grid,
         q, k, kt, v, lse, o, experts, slot_rows, scale):
    length, width = middle.shape
    heads = grid.shape[1]
    pairs = width // LANES
    smem = pl.BlockSpec(memory_space=pltpu.SMEM)
    vmem = pl.BlockSpec(memory_space=pltpu.VMEM)
    f32, bf16 = jnp.float32, jnp.bfloat16
    shape = jax.ShapeDtypeStruct
    act = shape((length, width), bf16)
    anywhere = pl.BlockSpec(memory_space=pl.ANY)
    return pl.pallas_call(
        functools.partial(back_kernel, experts=experts, slot_rows=slot_rows, scale=scale),
        out_shape=(act, act, act, shape((length, width), f32), shape(small_shape(width, experts), f32)),
        in_specs=[smem] * 2 + [vmem] * 13 + [anywhere] * 5,
        out_specs=(vmem, vmem, vmem, anywhere, vmem),
        scratch_shapes=[
            pltpu.VMEM((length, width), bf16),
            pltpu.VMEM((length, width), bf16),
            pltpu.VMEM((width, length), bf16),
            pltpu.VMEM((length, width), bf16),
            pltpu.VMEM((length, width), bf16),
            pltpu.VMEM((length, width), f32),
            pltpu.VMEM((length, width), bf16),
            pltpu.VMEM((length, LANES), bf16),
            pltpu.VMEM((length, LANES), bf16),
            pltpu.VMEM((16, 4 * LANES), f32),
            pltpu.VMEM((pairs, NEAR, BLOCK, 2 * LANES), f32),
            pltpu.VMEM((pairs, NEAR, BLOCK, 2 * LANES), f32),
            pltpu.VMEM((length, width), f32),
            pltpu.VMEM((length, width), f32),
            pltpu.VMEM((router_t.shape[0], length), f32),
            pltpu.VMEM((NEAR * 16, 2 * LANES), f32),
            pltpu.SemaphoreType.DMA((6,)),
        ],
        compiler_params=pltpu.CompilerParams(vmem_limit_bytes=63 << 20),
        cost_estimate=pl.CostEstimate(
            flops=10 * length * length * width + 6 * length * width * width, bytes_accessed=30 << 20,
            transcendentals=length * length * heads,
        ),
    )(lo, hi, home, home_gate, slot, routes_row, probs, middle, cotangent, segments, gain_two, wo, router_t, grid,
      lse, q, k, kt, v, o)


def finish_kernel(
    sum_q, sum_k, sum_v, sum_o, keep, passed, mixed_in, token_in, small,
    mixed_out, token_out, gain_one, gain_two, grad_q, grad_k, grad_v, grad_o, table_t, router_t, grad_in, grad_out,
    low, wide, load_sem, store_sem, copy_sem, *, experts,
):
    f32 = jnp.float32
    sources = (sum_o, sum_v, sum_k, sum_q, keep.at[0], keep.at[1], passed.at[0], passed.at[1])
    targets = (grad_o, grad_v, grad_k, grad_q, grad_in, grad_out)
    width = sum_q.shape[0]
    rows = 256
    spans = [pl.ds(r, rows) for r in range(0, width, rows)]
    copies = [
        pltpu.make_async_copy(mixed_in, mixed_out, copy_sem.at[0]),
        pltpu.make_async_copy(token_in, token_out, copy_sem.at[1]),
    ]
    loads = [
        [pltpu.make_async_copy(x.at[span], low.at[i, span], load_sem.at[i, j]) for j, span in enumerate(spans)]
        for i, x in enumerate(sources)
    ]
    stores = [
        [pltpu.make_async_copy(wide.at[i, span], x.at[span], store_sem.at[i, j]) for j, span in enumerate(spans)]
        for i, x in enumerate(targets)
    ]
    for i in range(8):
        for load in loads[i]:
            load.start()
    for copy in copies:
        copy.start()
    chunks = width // LANES
    gain_one[...] = jnp.concatenate([small[c : c + 1, :] for c in range(chunks)], 1).reshape(width)
    gain_two[...] = jnp.concatenate([small[8 + c : 9 + c, :] for c in range(chunks)], 1).reshape(width)
    for c in range(chunks):
        router_t[:, c * LANES : (c + 1) * LANES] = small[16 + c * experts : 16 + (c + 1) * experts, :]
    at = 16 + chunks * experts
    heads, buckets = table_t.shape
    table_t[...] = small[at : at + heads, :buckets]
    for i in range(4):
        for j, span in enumerate(spans):
            loads[i][j].wait()
            wide[i, span, :] = low[i, span, :].astype(f32)
            stores[i][j].start()
    for i in (4, 5):
        for j, span in enumerate(spans):
            loads[i][j].wait()
            loads[i + 2][j].wait()
            wide[i, span, :] = low[i, span, :].astype(f32) + low[i + 2, span, :].astype(f32)
            stores[i][j].start()
    for i in range(6):
        for store in stores[i]:
            store.wait()
    for copy in copies:
        copy.wait()


def finish(sums, keep, passed, mixed, token_grad, small, grid_shape, experts):
    f32, bf16 = jnp.float32, jnp.bfloat16
    width = sums[0].shape[0]
    vmem = pl.BlockSpec(memory_space=pltpu.VMEM)
    anywhere = pl.BlockSpec(memory_space=pl.ANY)
    shape = jax.ShapeDtypeStruct
    act = shape(mixed.shape, bf16)
    square, row = shape((width, width), f32), shape((width,), f32)
    blocks = width // 256
    return pl.pallas_call(
        functools.partial(finish_kernel, experts=experts),
        out_shape=(act, act, row, row, square, square, square, square, shape(grid_shape[::-1], f32),
                   shape((experts, width), f32), square, square),
        in_specs=[anywhere] * 8 + [vmem],
        out_specs=(anywhere,) * 2 + (vmem, vmem) + (anywhere,) * 4 + (vmem, vmem) + (anywhere,) * 2,
        scratch_shapes=[
            pltpu.VMEM((8, width, width), bf16), pltpu.VMEM((6, width, width), f32),
            pltpu.SemaphoreType.DMA((8, blocks)), pltpu.SemaphoreType.DMA((6, blocks)),
            pltpu.SemaphoreType.DMA((2,)),
        ],
        compiler_params=pltpu.CompilerParams(vmem_limit_bytes=63 << 20),
        cost_estimate=pl.CostEstimate(flops=0, bytes_accessed=30 << 20, transcendentals=0),
    )(*sums, keep, passed, mixed, token_grad, small)


def gelu_parts(v):
    mag = jnp.abs(v)
    t = 1.0 / (1.0 + (0.3275911 * 0.7071067811865476) * mag)
    poly = t * (0.127414796 + t * (-0.142248368 + t * (0.7107068705 + t * (-0.7265760135 + t * 0.5307027145))))
    gauss = jnp.exp(-0.5 * v * v)
    tail = poly * gauss
    phi = jnp.where(v < 0, tail, 1.0 - tail)
    return v * phi, phi + v * gauss * 0.3989422804014327


def flip_bits(index, mask, count):
    out = 0
    bit = 1
    while bit < count:
        a, b = (index // bit) % 2, (mask // bit) % 2
        out = out + bit * (a + b - 2 * a * b)
        bit *= 2
    return out


def ffn_kernel(
    xs, gs, g, win_hbm, wout_hbm,
    home, home_gate, produced, keep, give,
    win, wout, xr, gr, act, pg, gated, igs, ggs, dws, dwr, stage,
    wsem, own_sem, psem, ksem, xsend, xrecv, gsend, grecv, isend, irecv, qsend, qrecv, dsend, drecv,
    *, groups, dp_size, tiles,
):
    f32, bf16 = jnp.float32, jnp.bfloat16
    me = lax.axis_index("expert")
    dp = lax.axis_index("dp")
    core = dp % 2
    sibling = dp + 1 - 2 * core
    half_of = dp // 2
    rows = xs.shape[1]
    width = xs.shape[2]
    hidden = win.shape[1]
    tile = hidden // tiles
    lanes = gs.shape[2]

    def there(peer):
        return (dp, peer)

    load_in = pltpu.make_async_copy(win_hbm, win, wsem.at[0])
    load_out = pltpu.make_async_copy(wout_hbm, wout, wsem.at[1])
    load_in.start()
    load_out.start()
    load_g = pltpu.make_async_copy(g, gated, wsem.at[2])
    load_g.start()

    barrier = pltpu.get_barrier_semaphore()

    def greet(s, _):
        pl.semaphore_signal(
            barrier, inc=1, device_id=there(flip_bits(me, s, groups)), device_id_type=pl.DeviceIdType.MESH
        )
        return 0
    lax.fori_loop(1, groups, greet, 0)
    pl.semaphore_signal(barrier, inc=1, device_id=(sibling, me), device_id_type=pl.DeviceIdType.MESH)
    pl.semaphore_wait(barrier, groups)

    def x_copy(peer, slot):
        return pltpu.make_async_remote_copy(
            src_ref=xs.at[peer], dst_ref=xr.at[slot], send_sem=xsend.at[peer], recv_sem=xrecv.at[slot],
            device_id=there(peer), device_id_type=pl.DeviceIdType.MESH)

    def g_copy(peer, slot):
        return pltpu.make_async_remote_copy(
            src_ref=gs.at[peer], dst_ref=gr.at[slot], send_sem=gsend.at[peer], recv_sem=grecv.at[slot],
            device_id=there(peer), device_id_type=pl.DeviceIdType.MESH)

    def i_copy(peer, slot):
        return pltpu.make_async_remote_copy(
            src_ref=igs.at[peer], dst_ref=home.at[slot], send_sem=isend.at[peer], recv_sem=irecv.at[slot],
            device_id=there(peer), device_id_type=pl.DeviceIdType.MESH)

    def q_copy(peer, slot):
        return pltpu.make_async_remote_copy(
            src_ref=ggs.at[peer], dst_ref=home_gate.at[slot], send_sem=qsend.at[peer], recv_sem=qrecv.at[slot],
            device_id=there(peer), device_id_type=pl.DeviceIdType.MESH)

    def send(i, _):
        odd = (i - 1) % 2
        s = (1 - odd) * (groups - 1 - (i - 1) // 2) + odd * (i // 2)
        peer = flip_bits(me, s, groups)
        x_copy(peer, me).start()
        g_copy(peer, me).start()
        return 0
    lax.fori_loop(1, groups, send, 0)
    own_x = pltpu.make_async_copy(xs.at[me], xr.at[me], own_sem.at[0])
    own_g = pltpu.make_async_copy(gs.at[me], gr.at[me], own_sem.at[1])
    own_x.start()
    own_g.start()
    load_in.wait()
    load_out.wait()
    load_g.wait()

    spot = (
        lax.broadcasted_iota(jnp.int32, (rows, lanes), 0)
        == lax.broadcasted_iota(jnp.int32, (rows, lanes), 1)
    )

    def work(base):
        both = pl.ds(base, 2)
        x = xr[both].reshape(2 * rows, width)
        place = pl.ds(pl.multiple_of(base * rows, rows), 2 * rows)
        gg = gated[place, :]
        gate = jnp.concatenate(
            [jnp.sum(jnp.where(spot, gr[base + u, 0:1, :], 0.0), 1, keepdims=True) for u in range(2)], 0
        )
        gated[place, :] = (gate * gg.astype(f32)).astype(bf16)
        total = jnp.zeros((2 * rows, width), f32)
        gate_grad = jnp.zeros((2 * rows, 1), f32)

        def columns(t):
            return slice(t * tile, (t + 1) * tile)

        def products(t):
            return matmul(x, win[:, columns(t)]), matmul_nt(gg, wout[columns(t), :])

        ahead = products(0)
        for t in range(tiles):
            pre, out_grad = ahead
            if t + 1 < tiles:
                ahead = products(t + 1)
            value, slope = gelu_parts(pre)
            act[place, columns(t)] = value.astype(bf16)
            gate_grad = gate_grad + jnp.sum(value * out_grad, 1, keepdims=True)
            low = (gate * out_grad * slope).astype(bf16)
            pg[place, columns(t)] = low
            total = total + matmul_nt(low, win[:, columns(t)])
        igs[both] = total.astype(bf16).reshape(2, rows, width)
        for u in range(2):
            row = jnp.sum(jnp.where(spot, gate_grad[u * rows : (u + 1) * rows], 0.0), 0, keepdims=True)
            ggs[base + u] = jnp.broadcast_to(row, ggs.shape[1:])

    def arrive(peer):
        x_copy(peer, peer).wait_recv()
        g_copy(peer, peer).wait_recv()

    def back(peer):
        i_copy(peer, me).start()
        q_copy(peer, me).start()

    own_x.wait()
    own_g.wait()
    arrive(flip_bits(me, 1, groups))
    work(me - me % 2)
    own_i = pltpu.make_async_copy(igs.at[me], home.at[me], own_sem.at[0])
    own_q = pltpu.make_async_copy(ggs.at[me], home_gate.at[me], own_sem.at[1])
    own_i.start()
    own_q.start()
    back(flip_bits(me, 1, groups))

    def chunk(j, _):
        peer = flip_bits(me, 2 * j, groups)
        other = flip_bits(me, 2 * j + 1, groups)
        arrive(peer)
        arrive(other)
        work(peer - peer % 2)
        back(peer)
        back(other)
        return 0
    lax.fori_loop(1, groups // 2, chunk, 0)

    def d_copy(k):
        return pltpu.make_async_remote_copy(
            src_ref=dws.at[k % 2], dst_ref=dwr.at[k], send_sem=dsend.at[k], recv_sem=drecv.at[k],
            device_id=(sibling, me), device_id_type=pl.DeviceIdType.MESH)

    part = hidden // dp_size
    flat = groups * rows
    items = [(which, half) for half in (1 - half_of, half_of) for which in range(2)]

    def grad(which, quarter):
        span = pl.ds(pl.multiple_of(quarter * part, part), part)
        if which == 0:
            return matmul_tn(xr[...].reshape(flat, width), pg[:, span])
        return matmul_tn(act[:, span], gated[...])

    for k, (which, half) in enumerate(items):
        if k >= 2:
            d_copy(k - 2).wait_send()
        dws[k % 2] = grad(which, 2 * half + 1 - core).astype(bf16)
        d_copy(k).start()
    outs = [
        pltpu.make_async_copy(dwr.at[0], give.at[0], ksem.at[0]),
        pltpu.make_async_copy(dwr.at[1], give.at[1], ksem.at[1]),
        pltpu.make_async_copy(dwr.at[2], keep.at[0], ksem.at[2]),
        pltpu.make_async_copy(dwr.at[3], keep.at[1], ksem.at[3]),
    ]
    for k, (which, half) in enumerate(items):
        local = grad(which, 2 * half + core)
        d_copy(k).wait_recv()
        dwr[k] = (local + dwr[k].astype(f32)).astype(bf16)
        outs[k].start()

    span = stage.shape[1]
    copies = []
    for b in range(flat // span):
        if b >= 2:
            copies[b - 2].wait()
        stage[b % 2] = matmul(act[b * span : (b + 1) * span, :], wout[...]).astype(bf16)
        copy = pltpu.make_async_copy(stage.at[b % 2], produced.at[pl.ds(b * span, span)], psem.at[b % 2])
        copy.start()
        copies.append(copy)
    for copy in copies[-2:] + outs:
        copy.wait()
    own_i.wait()
    own_q.wait()
    for k in (2, 3):
        d_copy(k).wait_send()

    def finish(s, _):
        peer = flip_bits(me, s, groups)
        x_copy(peer, me).wait_send()
        g_copy(peer, me).wait_send()
        i_copy(peer, me).wait_send()
        q_copy(peer, me).wait_send()
        i_copy(peer, peer).wait_recv()
        q_copy(peer, peer).wait_recv()
        return 0
    lax.fori_loop(1, groups, finish, 0)


def ffn(xs, gs, g, weight_in, weight_out, groups, dp_size, tiles=6):
    f32, bf16 = jnp.float32, jnp.bfloat16
    _, rows, width = xs.shape
    hidden = weight_in.shape[1]
    lanes = gs.shape[2]
    part = hidden // dp_size
    anywhere = pl.BlockSpec(memory_space=pl.ANY)
    sem = pltpu.SemaphoreType.DMA
    flat = groups * rows
    shape = jax.ShapeDtypeStruct
    return pl.pallas_call(
        functools.partial(ffn_kernel, groups=groups, dp_size=dp_size, tiles=tiles),
        out_shape=(
            shape((groups, rows, width), bf16),
            shape((groups, 8, lanes), f32),
            shape((flat, width), bf16),
            shape((2, width, part), bf16),
            shape((2, width, part), bf16),
        ),
        in_specs=[anywhere] * 5,
        out_specs=(anywhere,) * 5,
        scratch_shapes=[
            pltpu.VMEM((width, hidden), bf16),
            pltpu.VMEM((hidden, width), bf16),
            pltpu.VMEM((groups, rows, width), bf16),
            pltpu.VMEM((groups, 8, lanes), f32),
            pltpu.VMEM((flat, hidden), bf16),
            pltpu.VMEM((flat, hidden), bf16),
            pltpu.VMEM((flat, width), bf16),
            pltpu.VMEM((groups, rows, width), bf16),
            pltpu.VMEM((groups, 8, lanes), f32),
            pltpu.VMEM((2, width, part), bf16),
            pltpu.VMEM((4, width, part), bf16),
            pltpu.VMEM((2, flat // 8, width), bf16),
            sem((3,)), sem((2,)), sem((2,)), sem((4,)),
            sem((groups,)), sem((groups,)), sem((groups,)), sem((groups,)),
            sem((groups,)), sem((groups,)), sem((groups,)), sem((groups,)),
            sem((4,)), sem((4,)),
        ],
        compiler_params=pltpu.CompilerParams(
            collective_id=1, has_side_effects=True, vmem_limit_bytes=62 << 20
        ),
        cost_estimate=pl.CostEstimate(
            flops=12 * flat * width * hidden, bytes_accessed=40 << 20, transcendentals=flat * hidden
        ),
    )(xs, gs, g, weight_in, weight_out)


def fold_steps(rows, cols, bits):
    steps = []
    for bit in bits[:3]:
        rows = rows // 2
        steps.append(((bit,), "half", rows, cols))
    rows, cols = rows // 2, cols // 2
    steps.append((tuple(bits[3:5]), "quad", rows, cols))
    for bit in bits[5:]:
        steps.append(((bit,), "whole", rows, cols))
    return steps


def reduce_kernel(
    attended_hbm, middle_grad_hbm, tokens_hbm, dv_hbm, dk_hbm, dq_hbm, wq_hbm, wk_hbm, wv_hbm, returned_hbm, middle_hbm,
    gain, small_in, slot_ref, routes_ref, probs_ref,
    sum_o, sum_v, sum_k, sum_q, token_grad_hbm, small_out, mixed_hbm,
    attended, middle_grad, tokens, dv, dk, dq, wq, wk, wv, returned, middle,
    token_grad, mixed, sums, normed, branch, acc, outbox, inbox, small_box, small_sent, load_sem, store_sem,
    ssend, srecv, tsend, trecv,
    *, dp_bits, expert_bits,
):
    f32, bf16 = jnp.float32, jnp.bfloat16
    dp = lax.axis_index("dp")
    ex = lax.axis_index("expert")
    MESH = pl.DeviceIdType.MESH
    length, width = tokens.shape
    held = (attended, middle_grad, tokens, dv, dk, dq, wq, wk, wv, returned, middle)
    loads = [
        pltpu.make_async_copy(there, here, load_sem.at[i])
        for i, (there, here) in enumerate(zip(
            (attended_hbm, middle_grad_hbm, tokens_hbm, dv_hbm, dk_hbm, dq_hbm, wq_hbm, wk_hbm, wv_hbm,
             returned_hbm, middle_hbm), held))
    ]
    first = 4
    for load in loads[:first]:
        load.start()

    def own_bit(bit):
        axis, place = bit
        return (dp // 2 ** place) % 2 if axis == "dp" else (ex // 2 ** place) % 2

    def partner(bits):
        there = [dp, ex]
        for bit in bits:
            there[bit[0] == "expert"] = there[bit[0] == "expert"] + (1 - 2 * own_bit(bit)) * 2 ** bit[1]
        return tuple(there)

    dpb = [("dp", i) for i in range(dp_bits)]
    exb = [("expert", i) for i in range(expert_bits)]
    orders = [
        [dpb[0], dpb[1], exb[0]] + dpb[2:] + exb[1:],
        [dpb[0], exb[0], dpb[1]] + dpb[2:] + exb[1:],
    ]
    every = dpb + exb
    small_count = len(every)

    barrier = pltpu.get_barrier_semaphore()
    greeted = [(bit,) for bit in every] + [tuple(orders[0][3:5])]
    for bits in greeted:
        pl.semaphore_signal(barrier, inc=1, device_id=partner(bits), device_id_type=MESH)
    pl.semaphore_wait(barrier, len(greeted))

    def prepare(i, _):
        span = pl.ds(pl.multiple_of(i * 256, 256), 256)
        x = tokens[span, :].astype(f32)
        inv = lax.rsqrt(jnp.mean(x * x, 1, keepdims=True) + epsilon)
        normed[span, :] = (x * inv * gain[...]).astype(bf16)
        branch[span, :] = middle_grad[span, :].astype(bf16)
        return 0
    for load in loads[:3]:
        load.wait()
    for load in loads[first:]:
        load.start()
    lax.fori_loop(0, length // 256, prepare, 0)

    lefts = (attended, normed, normed, normed)
    rights = (branch, dv, dk, dq)
    streams = []
    for s in range(4):
        row, col, at, sem_at = 0, 0, 0, 0
        plan = []
        for bits, kind, r, c in fold_steps(width, width, orders[s % 2]):
            mine = [own_bit(bit) for bit in bits]
            if kind == "half":
                peers = [bits]
                keep_at = (row + mine[0] * r, col)
                theirs = [(row + (1 - mine[0]) * r, col)]
            elif kind == "quad":
                peers = [bits[:1], bits[1:], bits]
                keep_at = (row + mine[0] * r, col + mine[1] * c)
                theirs = [
                    (row + (1 - mine[0]) * r, col + mine[1] * c),
                    (row + mine[0] * r, col + (1 - mine[1]) * c),
                    (row + (1 - mine[0]) * r, col + (1 - mine[1]) * c),
                ]
            else:
                peers, keep_at, theirs = [bits], (row, col), [(row, col)]
            plan.append((peers, kind, r, c, at, keep_at, theirs, sem_at))
            row, col = keep_at
            at += r * len(peers)
            sem_at += len(peers)
        streams.append(plan)
    count = len(streams[0])
    sems = ssend.shape[1] // 2

    def rs_copy(s, k, i):
        peers, kind, r, c, at, _, _, sem_at = streams[s][k]
        box = pl.ds(at + i * r, r)
        return pltpu.make_async_remote_copy(
            src_ref=outbox.at[s, box, pl.ds(0, c)], dst_ref=inbox.at[s, box, pl.ds(0, c)],
            send_sem=ssend.at[s, sem_at + i], recv_sem=srecv.at[s, sem_at + i],
            device_id=partner(peers[i]), device_id_type=MESH)

    def aligned(at):
        row, col = at
        row = pl.multiple_of(row, 16) if not isinstance(row, int) else row
        col = pl.multiple_of(col, 128) if not isinstance(col, int) else col
        return row, col

    def block(s, at, r, c):
        row, col = aligned(at)
        return sums.at[s, pl.ds(row, r), pl.ds(col, c)]

    def ag_copy(s, k, i, incoming):
        peers, kind, r, c, _, keep_at, theirs, sem_at = streams[s][k]
        ref = block(s, theirs[i] if incoming else keep_at, r, c)
        return pltpu.make_async_remote_copy(
            src_ref=ref, dst_ref=ref,
            send_sem=ssend.at[s, sems + sem_at + i], recv_sem=srecv.at[s, sems + sem_at + i],
            device_id=partner(peers[i]), device_id_type=MESH)

    half = width // 2
    core = own_bit(dpb[0])

    def grad(s, which):
        span = pl.ds(pl.multiple_of(which * half, half), half)
        return matmul_tn(lefts[s][:, span], rights[s][...])

    def local(s, at, r, c):
        row, col = aligned((at[0] - streams[s][0][5][0], at[1]))
        return acc.at[s, pl.ds(row, r), pl.ds(col, c)]

    def phase(s, k):
        plan = streams[s]
        if k == 0:
            if s > 0:
                loads[2 + s].wait()
            outbox[s, 0:half, :] = grad(s, 1 - core).astype(bf16)
            rs_copy(s, 0, 0).start()
            return
        if k <= count:
            peers, kind, r, c, at, keep_at, _, _ = plan[k - 1]
            view = local(s, keep_at, r, c)
            total = outbox[s, at : at + r, 0:c].astype(f32) if kind == "whole" else view[...]
            for i in range(len(peers)):
                rs_copy(s, k - 1, i).wait_recv()
                total = total + inbox[s, at + i * r : at + (i + 1) * r, 0:c].astype(f32)
            if k < count:
                view[...] = total
                peers, kind, r, c, at, _, theirs, _ = plan[k]
                for i in range(len(peers)):
                    outbox[s, at + i * r : at + (i + 1) * r, 0:c] = local(s, theirs[i], r, c)[...].astype(bf16)
                    rs_copy(s, k, i).start()
                return
            block(s, keep_at, r, c)[...] = total.astype(bf16)
        g = 2 * count - 1 - k
        if k > count and plan[g + 1][1] != "whole":
            for i in range(len(plan[g + 1][0])):
                ag_copy(s, g + 1, i, True).wait_recv()
        if g >= 0 and plan[g][1] != "whole":
            for i in range(len(plan[g][0])):
                ag_copy(s, g, i, False).start()

    gain_row = gain[...]
    rows = 256

    def norm_block(i, gain_grad):
        span = pl.ds(pl.multiple_of(i * rows, rows), rows)
        grads = (
            matmul_nt(dq[span, :], wq[...]) + matmul_nt(dk[span, :], wk[...]) + matmul_nt(dv[span, :], wv[...])
        )
        x = tokens[span, :].astype(f32)
        inv = lax.rsqrt(jnp.mean(x * x, 1, keepdims=True) + epsilon)
        scaled = grads * gain_row
        mean = jnp.sum(scaled * x, 1, keepdims=True) * (1.0 / width)
        part = inv * (scaled - x * (inv * inv * mean))
        token_grad[span, :] = (middle_grad[span, :] + part).astype(bf16)
        return gain_grad + jnp.sum(grads * (x * inv), 0, keepdims=True)

    slots = returned.shape[0]
    routes = routes_ref[...]
    pad = probs_ref.shape[0]
    hot = lax.broadcasted_iota(jnp.int32, (pad, length), 0) == routes
    gate_row = jnp.sum(jnp.where(hot, probs_ref[...], 0.0), 0, keepdims=True)

    def mix(c):
        at = slice(c, c + BLOCK)
        column = jnp.broadcast_to(slot_ref[0:1, at].astype(f32), (BLOCK, BLOCK)).T
        first = lax.broadcasted_iota(jnp.int32, (BLOCK, LANES), 1).astype(f32)
        spread = jnp.concatenate(
            [(column == first + float(s)).astype(f32).astype(bf16) for s in range(0, slots, LANES)], 1)
        rows_back = dot_nn(spread, returned[...])
        gate = jnp.broadcast_to(gate_row[:, at], (BLOCK, BLOCK)).T
        gate = jnp.concatenate([gate] * (width // LANES), 1)
        mixed[at, :] = (middle[at, :] + gate * rows_back).astype(bf16)

    def small_copy(k):
        return pltpu.make_async_remote_copy(
            src_ref=small_sent.at[k], dst_ref=small_box.at[k],
            send_sem=tsend.at[k], recv_sem=trecv.at[k],
            device_id=partner((every[k],)), device_id_type=MESH)

    def small_phase(k):
        if k == 0:
            gain_grad = lax.fori_loop(0, length // rows, norm_block, jnp.zeros((1, width), f32))
            small_out[...] = small_in[...]
            for i in range(width // LANES):
                small_out[i : i + 1, :] = gain_grad[:, i * LANES : (i + 1) * LANES]
        else:
            small_copy(k - 1).wait_recv()
            small_out[...] = small_out[...] + small_box[k - 1]
        if k < small_count:
            small_sent[k] = small_out[...]
            small_copy(k).start()

    last = 2 * count
    starts = (0, 0, 2, 2)
    stores = [
        pltpu.make_async_copy(sums.at[s], out, store_sem.at[s]) for s, out in enumerate((sum_o, sum_v, sum_k, sum_q))
    ]
    stores.append(pltpu.make_async_copy(token_grad, token_grad_hbm, store_sem.at[4]))
    stores.append(pltpu.make_async_copy(mixed, mixed_hbm, store_sem.at[5]))
    mixes = length // BLOCK
    turns = (1, 1, 4, 5, 6, 6, 8, 8)
    for t in range(max(last + starts[-1], small_count + 3, turns[-1]) + 1):
        for s in range(4):
            if 0 <= t - starts[s] <= last:
                phase(s, t - starts[s])
                if t - starts[s] == last:
                    stores[s].start()
        for s in range(4):
            if t == starts[s]:
                acc[s] = grad(s, core)
        if t == 3:
            for load in loads[6:9]:
                load.wait()
        if 0 <= t - 3 <= small_count:
            small_phase(t - 3)
            if t == 3:
                stores[4].start()
        if t == 1:
            for load in loads[9:]:
                load.wait()
        for c in range(mixes):
            if t == turns[c * len(turns) // mixes]:
                mix(c * BLOCK)
                if c == mixes - 1:
                    stores[5].start()
    for store in stores:
        store.wait()
    for s in range(4):
        for k in range(count):
            for i in range(len(streams[s][k][0])):
                rs_copy(s, k, i).wait_send()
                if streams[s][k][1] != "whole":
                    ag_copy(s, k, i, False).wait_send()
    for k in range(small_count):
        small_copy(k).wait_send()


def reduce_grads(tokens, attended, middle_grad, dq, dk, dv, wq, wk, wv, gain, small,
                 returned, slot, routes_row, probs, middle, dp_size, groups):
    f32, bf16 = jnp.float32, jnp.bfloat16
    length, width = tokens.shape
    dp_bits, expert_bits = dp_size.bit_length() - 1, groups.bit_length() - 1
    count = dp_bits + expert_bits
    steps = fold_steps(width, width, list(range(count)))
    box = sum(step[2] * (3 if step[1] == "quad" else 1) for step in steps)
    messages = sum(3 if step[1] == "quad" else 1 for step in steps)
    vmem = pl.BlockSpec(memory_space=pltpu.VMEM)
    anywhere = pl.BlockSpec(memory_space=pl.ANY)
    sem = pltpu.SemaphoreType.DMA
    shape = jax.ShapeDtypeStruct
    act, square = shape((length, width), bf16), shape((width, width), bf16)
    big = (attended, middle_grad, tokens, dv, dk, dq, wq, wk, wv, returned, middle)
    return pl.pallas_call(
        functools.partial(reduce_kernel, dp_bits=dp_bits, expert_bits=expert_bits),
        out_shape=(square, square, square, square, act, shape(small.shape, f32), act),
        in_specs=[anywhere] * len(big) + [vmem] * 5,
        out_specs=(anywhere,) * 5 + (vmem, anywhere),
        scratch_shapes=[pltpu.VMEM(x.shape, x.dtype) for x in big] + [
            pltpu.VMEM((length, width), bf16),
            pltpu.VMEM((length, width), bf16),
            pltpu.VMEM((4, width, width), bf16),
            pltpu.VMEM((length, width), bf16),
            pltpu.VMEM((length, width), bf16),
            pltpu.VMEM((4, width // 2, width), f32),
            pltpu.VMEM((4, box, width), bf16),
            pltpu.VMEM((4, box, width), bf16),
            pltpu.VMEM((count,) + small.shape, f32),
            pltpu.VMEM((count,) + small.shape, f32),
            sem((len(big),)), sem((6,)),
            sem((4, 2 * messages)), sem((4, 2 * messages)), sem((count,)), sem((count,)),
        ],
        compiler_params=pltpu.CompilerParams(
            collective_id=2, has_side_effects=True, vmem_limit_bytes=62 << 20
        ),
        cost_estimate=pl.CostEstimate(
            flops=14 * length * width * width, bytes_accessed=30 << 20, transcendentals=0
        ),
    )(*big, gain, small, slot, routes_row, probs)


def key_ranges(segment_row):
    first, last = segment_row[::BLOCK], segment_row[BLOCK - 1 :: BLOCK]
    lo = jnp.sum(segment_row[None, :] < first[:, None], 1) // BLOCK
    hi = (jnp.sum(segment_row[None, :] <= last[:, None], 1) + BLOCK - 1) // BLOCK
    return lo.astype(jnp.int32), hi.astype(jnp.int32)


def per_device(
    tokens,
    segments,
    routes,
    cotangent,
    attn_gain,
    ffn_gain,
    query_weight,
    key_weight,
    value_weight,
    output_weight,
    position_bias_grid,
    router_weight,
    expert_in,
    expert_out,
):
    f32, bf16 = jnp.float32, jnp.bfloat16
    token_count, model_width = tokens.shape
    head_count = position_bias_grid.shape[1]
    score_scale = (model_width // head_count) ** (-0.5)
    experts_all = router_weight.shape[1]
    capacity = (5 * token_count + 4 * experts_all - 1) // (4 * experts_all)
    slot_rows = (capacity + 15) // 16 * 16
    slots = experts_all * slot_rows
    groups = lax.axis_size("expert")
    dp_size = lax.axis_size("dp")

    def exchange(rows):
        return lax.all_to_all(rows, "expert", split_axis=0, concat_axis=0, tiled=True)

    routes_row = routes.reshape(1, token_count)
    token_slot, grad_slots = first_slots(routes_row, cotangent, experts_all, capacity, slot_rows)
    grad_arrived = exchange(grad_slots)
    lo, hi = key_ranges(segments[0])
    router_pad = max(experts_all, 16)
    router_t = jnp.pad(router_weight.T, ((0, router_pad - experts_all), (0, 0)))
    gain_one, gain_two = attn_gain[None, :], ffn_gain[None, :]
    queries, key_rows, keys_t, value_rows, attended, log_sums, middle, router_probs, sent, gate_slots = front(
        lo, hi, tokens, segments, token_slot, routes_row, gain_one, gain_two,
        query_weight, key_weight, value_weight, output_weight, position_bias_grid, router_t,
        experts_all, slot_rows, score_scale,
    )
    home_grad, home_gate, produced, keep, give = ffn(
        sent, gate_slots, grad_arrived.reshape(slots, model_width), expert_in[0], expert_out[0], groups, dp_size,
    )
    passed = lax.ppermute(give, "dp", [(i, (i + dp_size // 2) % dp_size) for i in range(dp_size)])
    returned = exchange(produced.reshape(experts_all, slot_rows, model_width)).reshape(slots, model_width)
    query_grad, key_grad, value_grad, middle_grad, small = back(
        lo, hi, home_grad, home_gate, token_slot, routes_row, router_probs, middle, cotangent, segments, gain_two,
        output_weight, router_t, position_bias_grid, queries, key_rows, keys_t, value_rows, log_sums, attended,
        experts_all, slot_rows, score_scale,
    )
    sum_o, sum_v, sum_k, sum_q, token_grad, small, mixed = reduce_grads(
        tokens, attended, middle_grad, query_grad, key_grad, value_grad,
        query_weight, key_weight, value_weight, gain_one, small,
        returned, token_slot, routes_row, router_probs, middle, dp_size, groups,
    )
    (mixed, token_grad, attn_gain_grad, ffn_gain_grad, grad_q, grad_k, grad_v, grad_o, table_grad, router_grad,
     grad_in, grad_out) = finish(
        (sum_q, sum_k, sum_v, sum_o), keep, passed, mixed, token_grad, small, position_bias_grid.shape, experts_all
    )
    return (
        mixed,
        token_grad,
        attn_gain_grad,
        ffn_gain_grad,
        grad_q,
        grad_k,
        grad_v,
        grad_o,
        table_grad.T,
        router_grad.T,
        grad_in[None],
        grad_out[None],
    )


def solution(mesh):
    rows = P(("dp", "expert"), None)
    return jax.shard_map(
        per_device,
        mesh=mesh,
        in_specs=(rows,) * 4 + (P(),) * 8 + (P("expert", None, None),) * 2,
        out_specs=(rows,) * 2 + (P(),) * 8 + (P("expert", None, "dp"), P("expert", "dp", None)),
        check_vma=False,
    )
```

profile of v0, /device:TPU:1, one launch (start us, length us, event | category | flops | bytes accessed | tf_op | source)
XLA Modules:
  0.0 363.2 jit_solution(2105448687450810587)
XLA Ops:
  0.6 5.1 %shard_map.229 = (s32[8,1024]{1,0:T(8,128)}, bf16[8,160,768]{2,1,0:T(8,128)(2,1)}) custom-call(s32[1,1024]{1,0:T(1,128)} %bitcast.23, bf16[1024,768]{1,0:T(8,128)(2,1)} %cotangent.1), custom_call_target="tpu_custom_call" | custom-call | flops 2013265920 | bytes 4194304 | tf_op jit(solution)/shard_map/pallas_call | solution.py:310
  5.7 0.0 copy-start.4
  5.7 0.0 copy-start.2
  5.7 0.0 copy-start.3
  5.7 0.0 copy-start.1
  5.7 0.0 copy-start
  5.7 6.5 %all-to-all-start = ((bf16[8,160,768]{2,1,0:T(8,128)(2,1)}), bf16[8,160,768]{2,1,0:T(8,128)(2,1)}, u32[]{:S(2)}, u32[]{:S(2)}) async-start(bf16[8,160,768]{2,1,0:T(8,128)(2,1)} %get-tuple-element.57), calls=%async_computation | async-start | bytes 3932160 | tf_op jit(solution)/shard_map/all_to_all | solution.py:1299
  12.3 0.0 copy-done.4
  12.3 0.1 slice.7
  12.4 0.1 slice.6
  12.5 0.0 copy-done.2
  12.5 0.6 broadcast_in_dim.14.gain_one.gain
  13.0 0.0 copy-done.3
  13.0 0.6 broadcast_in_dim.15.gain_two
  13.6 0.0 copy-done.1
  13.6 0.7 copy.28.grid_ref
  14.3 0.0 copy-done
  14.3 0.6 pad.4.router_t
  14.9 0.2 convert_reduce_fusion
  15.2 0.6 and_select_fusion
  15.8 30.0 %shard_map.230 = (bf16[1024,768]{1,0:T(8,128)(2,1)}, bf16[1024,768]{1,0:T(8,128)(2,1)}, bf16[768,1024]{1,0:T(8,128)(2,1)}, bf16[1024,768]{1,0:T(8,128)(2,1)}, bf...) custom-call(s32[8]{0:T(128)} %get-tuple-element.97.lo_ref, ...), custom_call_target="tpu_custom_call" | custom-call | flops 10468982784 | bytes 20971520 | tf_op jit(solution)/shard_map/pallas_call | solution.py:424
  45.7 11.2 %all-to-all-done = bf16[8,160,768]{2,1,0:T(8,128)(2,1)} async-done(((bf16[8,160,768]{2,1,0:T(8,128)(2,1)}), bf16[8,160,768]{2,1,0:T(8,128)(2,1)}, u32[]{:S(2)}, u32[]{:S(2)}) %all-to-all-start) | async-done | bytes 1966112 | tf_op jit(solution)/shard_map/all_to_all | solution.py:1299
  56.9 90.8 %shard_map.231 = (bf16[8,160,768]{2,1,0:T(8,128)(2,1)}, f32[8,8,256]{2,1,0:T(8,128)}, bf16[1280,768]{1,0:T(8,128)(2,1)}, bf16[2,768,768]{2,1,0:T(8,128)(2,1)}, bf16[2,768,768]{2,1,0:T(8,128)(2,1)}) custom-call(bf16[8,160,768]{2,1,0:T(8,128)(2,1)} %get-tuple-element.55.xs, f32[8,8,256]{2,1,0:T(8,128)} %get-tuple-element.56.gs, bf16[1280,768]{1,0:T(8,128)(2,1)} %bitcast.3.g, ...), custom_call_target="tpu_custom_call" | custom-call | flops 36238786560 | bytes 41943040 | tf_op jit(solution)/shard_map/pallas_call | solution.py:913
  147.7 4.4 %all-to-all-start.1 = ((bf16[8,160,768]{2,1,0:T(8,128)(2,1)}), bf16[8,160,768]{2,1,0:T(8,128)(2,1)}, u32[]{:S(2)}, u32[]{:S(2)}) async-start(bf16[8,160,768]{2,1,0:T(8,128)(2,1)} %bitcast.12), calls=%async_computation.1 | async-start | bytes 3932160 | tf_op jit(solution)/shard_map/all_to_all | solution.py:1299
  152.1 1.3 collective-permute-start
  153.4 41.0 %shard_map.232 = (bf16[1024,768]{1,0:T(8,128)(2,1)}, bf16[1024,768]{1,0:T(8,128)(2,1)}, bf16[1024,768]{1,0:T(8,128)(2,1)}, f32[1024,768]{1,0:T(8,128)}, f32[80,128]{1,0:T(8,128)}) custom-call(s32[8]{0:T(128)} %get-tuple-element.97.lo_ref, s32[8]{0:T(128)} %get-tuple-element.96.hi_ref, bf16[8,160,768]{2,1,0:T(8,128)(2,1)} %get-tuple-element.58.home, ...), custom_call_target="tpu_custom_call" | custom-call | flops 11676942336 | bytes 31457280 | tf_op jit(solution)/shard_map/pallas_call | solution.py:567
  194.5 1.7 all-to-all-done.1
  196.2 68.5 %shard_map.233 = (bf16[768,768]{1,0:T(8,128)(2,1)}, bf16[768,768]{1,0:T(8,128)(2,1)}, bf16[768,768]{1,0:T(8,128)(2,1)}, bf16[768,768]{1,0:T(8,128)(2,1)}, bf16[1...) custom-call(bf16[1024,768]{1,0:T(8,128)(2,1)} %get-tuple-element.54.o_hbm.attended_hbm, ...), custom_call_target="tpu_custom_call" | custom-call | flops 8455716864 | bytes 31457280 | tf_op jit(solution)/shard_map/pallas_call | solution.py:1236
  264.7 0.0 collective-permute-done.passed
  264.7 98.2 %shard_map.234 = (bf16[1024,768]{1,0:T(8,128)(2,1)}, bf16[1024,768]{1,0:T(8,128)(2,1)}, f32[768]{0:T(1024)}, f32[768]{0:T(1024)}, f32[768,768]{1,0:T(8,128)}, /*...) custom-call(bf16[768,768]{1,0:T(8,128)(2,1)} %get-tuple-element.73.s, ...), custom_call_target="tpu_custom_call" | custom-call | bytes 31457280 | tf_op jit(solution)/shard_map/pallas_call | solution.py:663
Async XLA Ops:
  5.7 6.6 %copy-start.4 = (s32[1,1024]{1,0:T(1,128)S(1)}, s32[1,1024]{1,0:T(1,128)}, u32[]{:S(2)}) copy-start(s32[1,1024]{1,0:T(1,128)} %segment_row.3) | copy-start | bytes 12292
  5.7 6.7 %copy-start.2 = (f32[768]{0:T(1024)S(1)}, f32[768]{0:T(1024)}, u32[]{:S(2)}) copy-start(f32[768]{0:T(1024)} %param.18) | copy-start | bytes 9220
  5.7 7.3 %copy-start.3 = (f32[768]{0:T(1024)S(1)}, f32[768]{0:T(1024)}, u32[]{:S(2)}) copy-start(f32[768]{0:T(1024)} %param.19) | copy-start | bytes 9220
  5.7 7.9 %copy-start.1 = (f32[32,12]{0,1:T(8,128)S(1)}, f32[32,12]{0,1:T(8,128)}, u32[]{:S(2)}) copy-start(f32[32,12]{0,1:T(8,128)} %param.24) | copy-start | bytes 4612
  5.7 8.6 %copy-start = (f32[768,8]{0,1:T(8,128)S(1)}, f32[768,8]{0,1:T(8,128)}, u32[]{:S(2)}) copy-start(f32[768,8]{0,1:T(8,128)} %param.25) | copy-start | bytes 73732
  5.7 51.2 %all-to-all-start = ((bf16[8,160,768]{2,1,0:T(8,128)(2,1)}), bf16[8,160,768]{2,1,0:T(8,128)(2,1)}, u32[]{:S(2)}, u32[]{:S(2)}) async-start(bf16[8,160,768]{2,1,0:T(8,128)(2,1)} %get-tuple-element.57), calls=%async_computation | async-start | bytes 3932160 | tf_op jit(solution)/shard_map/all_to_all | solution.py:1299
  147.7 48.5 %all-to-all-start.1 = ((bf16[8,160,768]{2,1,0:T(8,128)(2,1)}), bf16[8,160,768]{2,1,0:T(8,128)(2,1)}, u32[]{:S(2)}, u32[]{:S(2)}) async-start(bf16[8,160,768]{2,1,0:T(8,128)(2,1)} %bitcast.12), calls=%async_computation.1 | async-start | bytes 3932160 | tf_op jit(solution)/shard_map/all_to_all | solution.py:1299
  152.1 112.6 %collective-permute-start = (bf16[2,768,768]{2,1,0:T(8,128)(2,1)}, bf16[2,768,768]{2,1,0:T(8,128)(2,1)}, u32[]{:S(2)}, u32[]{:S(2)}) collective-permute-start(bf16[2,768,768]{2,1,0:T(8,128)(2,1)} %get-tuple-element.78), channel_id=1, source_target_pairs={{0,16},{8,24},{16,0},{24,8},{1,17},{9,25},{17,1},{25,9},{2,18},{10... | collective-permute-start | bytes 7077896 | tf_op jit(solution)/shard_map/ppermute | solution.py:1316
where the time goes:
time: 369 us; the launch traced here: 363 us
  Pallas kernels  334 us (91%)
  waiting for transfers between devices  12.9 us (3%)
  starting transfers between devices  12.2 us (3%)
    pallas_call x1, Pallas kernels, finish(): pl.pallas_call(functools.partial(finish_kernel, experts=experts), out_sha...  98.2 us
    pallas_call x1, Pallas kernels, ffn(): pl.pallas_call(functools.partial(ffn_kernel, groups=groups, dp_size=dp_si...  90.8 us
    pallas_call x1, Pallas kernels, reduce_grads(): pl.pallas_call(functools.partial(reduce_kernel, dp_bits=dp_bits, expert_b...  68.5 us
    pallas_call x1, Pallas kernels, back(): pl.pallas_call(functools.partial(back_kernel, experts=experts, slot_rows=...  41 us
    pallas_call x1, Pallas kernels, front(): pl.pallas_call(functools.partial(front_kernel, experts=experts, slot_rows...  30 us
    all_to_all x2, waiting for transfers between devices, exchange(): lax.all_to_all(rows, 'expert', split_axis=0, concat_axis=0, tiled=True)  12.9 us
    all_to_all x2, starting transfers between devices, exchange(): lax.all_to_all(rows, 'expert', split_axis=0, concat_axis=0, tiled=True)  10.9 us
  transfers between devices with their start and end apart: 3, of which 2 were waited for; matrix products, arithmetic and copies ran while one was open for 1% of the time, Pallas kernels for 38%

commit v1 on v0

--- a/solution.py
+++ b/solution.py
@@ -600,7 +600,7 @@
 def finish_kernel(
     sum_q, sum_k, sum_v, sum_o, keep, passed, mixed_in, token_in, small,
     mixed_out, token_out, gain_one, gain_two, grad_q, grad_k, grad_v, grad_o, table_t, router_t, grad_in, grad_out,
-    low, wide, load_sem, store_sem, copy_sem, *, experts,
+    low, wide, through, load_sem, store_sem, copy_sem, *, experts,
 ):
     f32 = jnp.float32
     sources = (sum_o, sum_v, sum_k, sum_q, keep.at[0], keep.at[1], passed.at[0], passed.at[1])
@@ -608,9 +608,11 @@
     width = sum_q.shape[0]
     rows = 256
     spans = [pl.ds(r, rows) for r in range(0, width, rows)]
+    fetches = [
+        pltpu.make_async_copy(x, through.at[i], copy_sem.at[i]) for i, x in enumerate((mixed_in, token_in))
+    ]
     copies = [
-        pltpu.make_async_copy(mixed_in, mixed_out, copy_sem.at[0]),
-        pltpu.make_async_copy(token_in, token_out, copy_sem.at[1]),
+        pltpu.make_async_copy(through.at[i], x, copy_sem.at[2 + i]) for i, x in enumerate((mixed_out, token_out))
     ]
     loads = [
         [pltpu.make_async_copy(x.at[span], low.at[i, span], load_sem.at[i, j]) for j, span in enumerate(spans)]
@@ -620,11 +622,14 @@
         [pltpu.make_async_copy(wide.at[i, span], x.at[span], store_sem.at[i, j]) for j, span in enumerate(spans)]
         for i, x in enumerate(targets)
     ]
-    for i in range(8):
+    for i in range(4):
         for load in loads[i]:
             load.start()
-    for copy in copies:
-        copy.start()
+    for fetch in fetches:
+        fetch.start()
+    for i in range(4, 8):
+        for load in loads[i]:
+            load.start()
     chunks = width // LANES
     gain_one[...] = jnp.concatenate([small[c : c + 1, :] for c in range(chunks)], 1).reshape(width)
     gain_two[...] = jnp.concatenate([small[8 + c : 9 + c, :] for c in range(chunks)], 1).reshape(width)
@@ -638,6 +643,9 @@
             loads[i][j].wait()
             wide[i, span, :] = low[i, span, :].astype(f32)
             stores[i][j].start()
+    for fetch, copy in zip(fetches, copies):
+        fetch.wait()
+        copy.start()
     for i in (4, 5):
         for j, span in enumerate(spans):
             loads[i][j].wait()
@@ -668,8 +676,9 @@
         out_specs=(anywhere,) * 2 + (vmem, vmem) + (anywhere,) * 4 + (vmem, vmem) + (anywhere,) * 2,
         scratch_shapes=[
             pltpu.VMEM((8, width, width), bf16), pltpu.VMEM((6, width, width), f32),
+            pltpu.VMEM((2,) + mixed.shape, bf16),
             pltpu.SemaphoreType.DMA((8, blocks)), pltpu.SemaphoreType.DMA((6, blocks)),
-            pltpu.SemaphoreType.DMA((2,)),
+            pltpu.SemaphoreType.DMA((4,)),
         ],
         compiler_params=pltpu.CompilerParams(vmem_limit_bytes=63 << 20),
         cost_estimate=pl.CostEstimate(flops=0, bytes_accessed=30 << 20, transcendentals=0),

time: 369 us -> 282 us (0.76)
  Pallas kernels: 334 us -> 248 us
    pallas_call x1, Pallas kernels: 98.2 us -> 12.3 us  [finish(): pl.pallas_call(functools.partial(finish_kernel, experts=experts), out_sha...]
  transfers between devices with their start and end apart: 3 -> 3, of which waited for: 2 -> 2; matrix products, arithmetic and copies ran while one was open for 1% -> 1% of each run, Pallas kernels for 38% -> 50%
where the time goes in v1:
time: 282 us; the launch traced here: 277 us
  Pallas kernels  248 us (88%)
  waiting for transfers between devices  12.5 us (4%)
  starting transfers between devices  12.2 us (4%)
    pallas_call x1, Pallas kernels, ffn(): pl.pallas_call(functools.partial(ffn_kernel, groups=groups, dp_size=dp_si...  90.8 us
    pallas_call x1, Pallas kernels, reduce_grads(): pl.pallas_call(functools.partial(reduce_kernel, dp_bits=dp_bits, expert_b...  68.3 us
    pallas_call x1, Pallas kernels, back(): pl.pallas_call(functools.partial(back_kernel, experts=experts, slot_rows=...  41.3 us
    pallas_call x1, Pallas kernels, front(): pl.pallas_call(functools.partial(front_kernel, experts=experts, slot_rows...  30.2 us
    all_to_all x2, waiting for transfers between devices, exchange(): lax.all_to_all(rows, 'expert', split_axis=0, concat_axis=0, tiled=True)  12.5 us
    pallas_call x1, Pallas kernels, finish(): pl.pallas_call(functools.partial(finish_kernel, experts=experts), out_sha...  12.3 us
    all_to_all x2, starting transfers between devices, exchange(): lax.all_to_all(rows, 'expert', split_axis=0, concat_axis=0, tiled=True)  10.9 us
  transfers between devices with their start and end apart: 3, of which 2 were waited for; matrix products, arithmetic and copies ran while one was open for 1% of the time, Pallas kernels for 50%

profile of v1, /device:TPU:1, one launch (start us, length us, event | category | flops | bytes accessed | tf_op | source)
XLA Modules:
  0.0 277.1 jit_solution(16154386536091389276)
XLA Ops:
  0.6 5.1 %shard_map.229 = (s32[8,1024]{1,0:T(8,128)}, bf16[8,160,768]{2,1,0:T(8,128)(2,1)}) custom-call(s32[1,1024]{1,0:T(1,128)} %bitcast.23, bf16[1024,768]{1,0:T(8,128)(2,1)} %cotangent.1), custom_call_target="tpu_custom_call" | custom-call | flops 2013265920 | bytes 4194304 | tf_op jit(solution)/shard_map/pallas_call | solution.py:310
  5.7 0.0 copy-start.4
  5.7 0.0 copy-start.2
  5.7 0.0 copy-start.3
  5.7 0.0 copy-start.1
  5.7 0.0 copy-start
  5.7 6.5 %all-to-all-start = ((bf16[8,160,768]{2,1,0:T(8,128)(2,1)}), bf16[8,160,768]{2,1,0:T(8,128)(2,1)}, u32[]{:S(2)}, u32[]{:S(2)}) async-start(bf16[8,160,768]{2,1,0:T(8,128)(2,1)} %get-tuple-element.57), calls=%async_computation | async-start | bytes 3932160 | tf_op jit(solution)/shard_map/all_to_all | solution.py:1308
  12.3 0.0 copy-done.4
  12.3 0.1 slice.7
  12.4 0.1 slice.6
  12.5 0.0 copy-done.2
  12.5 0.6 broadcast_in_dim.14.gain_one.gain
  13.0 0.0 copy-done.3
  13.0 0.6 broadcast_in_dim.15.gain_two
  13.6 0.0 copy-done.1
  13.6 0.7 copy.28.grid_ref
  14.3 0.0 copy-done
  14.3 0.6 pad.4.router_t
  14.9 0.2 convert_reduce_fusion
  15.2 0.6 and_select_fusion
  15.8 30.2 %shard_map.230 = (bf16[1024,768]{1,0:T(8,128)(2,1)}, bf16[1024,768]{1,0:T(8,128)(2,1)}, bf16[768,1024]{1,0:T(8,128)(2,1)}, bf16[1024,768]{1,0:T(8,128)(2,1)}, bf...) custom-call(s32[8]{0:T(128)} %get-tuple-element.97.lo_ref, ...), custom_call_target="tpu_custom_call" | custom-call | flops 10468982784 | bytes 20971520 | tf_op jit(solution)/shard_map/pallas_call | solution.py:424
  45.9 11.0 %all-to-all-done = bf16[8,160,768]{2,1,0:T(8,128)(2,1)} async-done(((bf16[8,160,768]{2,1,0:T(8,128)(2,1)}), bf16[8,160,768]{2,1,0:T(8,128)(2,1)}, u32[]{:S(2)}, u32[]{:S(2)}) %all-to-all-start) | async-done | bytes 1966112 | tf_op jit(solution)/shard_map/all_to_all | solution.py:1308
  56.9 90.8 %shard_map.231 = (bf16[8,160,768]{2,1,0:T(8,128)(2,1)}, f32[8,8,256]{2,1,0:T(8,128)}, bf16[1280,768]{1,0:T(8,128)(2,1)}, bf16[2,768,768]{2,1,0:T(8,128)(2,1)}, bf16[2,768,768]{2,1,0:T(8,128)(2,1)}) custom-call(bf16[8,160,768]{2,1,0:T(8,128)(2,1)} %get-tuple-element.55.xs, f32[8,8,256]{2,1,0:T(8,128)} %get-tuple-element.56.gs, bf16[1280,768]{1,0:T(8,128)(2,1)} %bitcast.3.g, ...), custom_call_target="tpu_custom_call" | custom-call | flops 36238786560 | bytes 41943040 | tf_op jit(solution)/shard_map/pallas_call | solution.py:922
  147.7 4.4 %all-to-all-start.1 = ((bf16[8,160,768]{2,1,0:T(8,128)(2,1)}), bf16[8,160,768]{2,1,0:T(8,128)(2,1)}, u32[]{:S(2)}, u32[]{:S(2)}) async-start(bf16[8,160,768]{2,1,0:T(8,128)(2,1)} %bitcast.12), calls=%async_computation.1 | async-start | bytes 3932160 | tf_op jit(solution)/shard_map/all_to_all | solution.py:1308
  152.1 1.3 collective-permute-start
  153.4 41.3 %shard_map.232 = (bf16[1024,768]{1,0:T(8,128)(2,1)}, bf16[1024,768]{1,0:T(8,128)(2,1)}, bf16[1024,768]{1,0:T(8,128)(2,1)}, f32[1024,768]{1,0:T(8,128)}, f32[80,128]{1,0:T(8,128)}) custom-call(s32[8]{0:T(128)} %get-tuple-element.97.lo_ref, s32[8]{0:T(128)} %get-tuple-element.96.hi_ref, bf16[8,160,768]{2,1,0:T(8,128)(2,1)} %get-tuple-element.58.home, ...), custom_call_target="tpu_custom_call" | custom-call | flops 11676942336 | bytes 31457280 | tf_op jit(solution)/shard_map/pallas_call | solution.py:567
  194.7 1.5 all-to-all-done.1
  196.2 68.3 %shard_map.233 = (bf16[768,768]{1,0:T(8,128)(2,1)}, bf16[768,768]{1,0:T(8,128)(2,1)}, bf16[768,768]{1,0:T(8,128)(2,1)}, bf16[768,768]{1,0:T(8,128)(2,1)}, bf16[1...) custom-call(bf16[1024,768]{1,0:T(8,128)(2,1)} %get-tuple-element.54.o_hbm.attended_hbm, ...), custom_call_target="tpu_custom_call" | custom-call | flops 8455716864 | bytes 31457280 | tf_op jit(solution)/shard_map/pallas_call | solution.py:1245
  264.6 0.0 collective-permute-done.passed
  264.6 12.3 %shard_map.234 = (bf16[1024,768]{1,0:T(8,128)(2,1)}, bf16[1024,768]{1,0:T(8,128)(2,1)}, f32[768]{0:T(1024)}, f32[768]{0:T(1024)}, f32[768,768]{1,0:T(8,128)}, /*...) custom-call(bf16[768,768]{1,0:T(8,128)(2,1)} %get-tuple-element.73.s, ...), custom_call_target="tpu_custom_call" | custom-call | bytes 31457280 | tf_op jit(solution)/shard_map/pallas_call | solution.py:671
Async XLA Ops:
  5.7 6.6 %copy-start.4 = (s32[1,1024]{1,0:T(1,128)S(1)}, s32[1,1024]{1,0:T(1,128)}, u32[]{:S(2)}) copy-start(s32[1,1024]{1,0:T(1,128)} %segment_row.3) | copy-start | bytes 12292
  5.7 6.7 %copy-start.2 = (f32[768]{0:T(1024)S(1)}, f32[768]{0:T(1024)}, u32[]{:S(2)}) copy-start(f32[768]{0:T(1024)} %param.18) | copy-start | bytes 9220
  5.7 7.3 %copy-start.3 = (f32[768]{0:T(1024)S(1)}, f32[768]{0:T(1024)}, u32[]{:S(2)}) copy-start(f32[768]{0:T(1024)} %param.19) | copy-start | bytes 9220
  5.7 7.9 %copy-start.1 = (f32[32,12]{0,1:T(8,128)S(1)}, f32[32,12]{0,1:T(8,128)}, u32[]{:S(2)}) copy-start(f32[32,12]{0,1:T(8,128)} %param.24) | copy-start | bytes 4612
  5.7 8.6 %copy-start = (f32[768,8]{0,1:T(8,128)S(1)}, f32[768,8]{0,1:T(8,128)}, u32[]{:S(2)}) copy-start(f32[768,8]{0,1:T(8,128)} %param.25) | copy-start | bytes 73732
  5.7 51.2 %all-to-all-start = ((bf16[8,160,768]{2,1,0:T(8,128)(2,1)}), bf16[8,160,768]{2,1,0:T(8,128)(2,1)}, u32[]{:S(2)}, u32[]{:S(2)}) async-start(bf16[8,160,768]{2,1,0:T(8,128)(2,1)} %get-tuple-element.57), calls=%async_computation | async-start | bytes 3932160 | tf_op jit(solution)/shard_map/all_to_all | solution.py:1308
  147.7 48.5 %all-to-all-start.1 = ((bf16[8,160,768]{2,1,0:T(8,128)(2,1)}), bf16[8,160,768]{2,1,0:T(8,128)(2,1)}, u32[]{:S(2)}, u32[]{:S(2)}) async-start(bf16[8,160,768]{2,1,0:T(8,128)(2,1)} %bitcast.12), calls=%async_computation.1 | async-start | bytes 3932160 | tf_op jit(solution)/shard_map/all_to_all | solution.py:1308
  152.1 112.4 %collective-permute-start = (bf16[2,768,768]{2,1,0:T(8,128)(2,1)}, bf16[2,768,768]{2,1,0:T(8,128)(2,1)}, u32[]{:S(2)}, u32[]{:S(2)}) collective-permute-start(bf16[2,768,768]{2,1,0:T(8,128)(2,1)} %get-tuple-element.78), channel_id=1, source_target_pairs={{0,16},{8,24},{16,0},{24,8},{1,17},{9,25},{17,1},{25,9},{2,18},{10... | collective-permute-start | bytes 7077896 | tf_op jit(solution)/shard_map/ppermute | solution.py:1325
